TPU v7x, 512 devices: a whole 4x8x8 slice. The times are simulated.
512 devices in a mesh: dom: 128 (over z, y, core), rep: 4 (over x).
Axes of the slice: x: 4, y: 8, z: 8, core: 2. Of those that a mesh axis runs over, the one named last changes fastest.
Arguments:
- features: bfloat16 [262144, 768], P(('dom', 'rep')), may hold values from -13 to 13
- sketch_matrix: bfloat16 [768, 256], replicated, may hold values from -0.21875 to 0.21875
- tiles: bfloat16 [128, 20, 256, 256], P('dom'), may hold values from 0 to 2, as said below
- tile_dst: int32 [128, 20], P('dom'), may hold values from -1 to 7, as said below
- tile_src: int32 [128, 20], P('dom'), may hold values from 0 to 11, as said below
- halo_index: int32 [128, 1024], P('dom'), may hold values from 0 to 2047
- send_order: int32 [128, 2048], P('dom'), may hold values from 0 to 2047, each once within a row
- arrival_place: int32 [128, 2048], P('dom'), may hold values from 0 to 2047, each once within a row
Outputs:
- signals: bfloat16 [3, 256, 262144], P(None, 'rep', 'dom')
Inputs may be any that keep to these rules, and one draw needn't show every extreme that they name: `tiles`: entries are zero or positive; in slot t < 8 of every partition the tile's diagonal is positive. `tile_dst`: in every partition slot t < 8 holds t, the live slots come first and the others hold -1; some partition uses every slot and some only the first 12. `tile_src`: slot t < 12 holds t in every partition; empty slots hold 0. `halo_index`: A row may be listed for several peers and more than once. `send_order`: each row is a permutation. `arrival_place`: each row is a permutation.
All inputs are finite; a program needn't handle non-finite values.
Results may differ from a plain program's by a relative error of at most 0.0034.
Values may be sent and summed in bfloat16 or wider, within the bound.
A program may use at most 64 MiB of HBM per device.

v0:
```python
import jax
import jax.numpy as jnp
from jax import lax
from jax.sharding import PartitionSpec as P


def on_device(
    features, sketch_matrix, tiles, tile_dst, tile_src, halo_index, send_order, arrival_place
):
    sketched = lax.dot_general(
        sketch_matrix, features, (((0,), (1,)), ((), ())), preferred_element_type=jnp.float32
    ).astype(jnp.bfloat16)
    hop0 = lax.all_to_all(sketched, "rep", split_axis=0, concat_axis=1, tiled=True)
    tile_set = tiles[0]
    targets = tile_dst[0]
    sources = tile_src[0]
    halo_rows = halo_index[0]
    order = send_order[0]
    place = arrival_place[0]
    channels, node_count = hop0.shape
    tile_size = tile_set.shape[-1]
    block_count = node_count // tile_size
    onehot = (targets[:, None] == jnp.arange(block_count, dtype=jnp.int32)[None, :]).astype(
        jnp.float32
    )
    row_sums = jnp.sum(tile_set, axis=2, dtype=jnp.float32)
    degree = jnp.einsum("ti,tb->bi", row_sums, onehot, precision=lax.Precision.HIGHEST).reshape(
        node_count
    )

    def combine(layer, received):
        columns = jnp.concatenate([layer, received], 1)
        blocks = columns.reshape(channels, -1, tile_size)[:, sources, :]
        products = jnp.einsum("ctj,tij->cti", blocks, tile_set, preferred_element_type=jnp.float32)
        summed = jnp.einsum("cti,tb->cbi", products, onehot, precision=lax.Precision.HIGHEST)
        summed = summed.reshape(channels, node_count)
        return (summed / degree[None, :]).astype(jnp.bfloat16)

    hop1 = combine(
        hop0, lax.all_to_all(hop0[:, halo_rows], "dom", split_axis=1, concat_axis=1, tiled=True)
    )
    hop2 = combine(
        hop1, lax.all_to_all(hop1[:, halo_rows], "dom", split_axis=1, concat_axis=1, tiled=True)
    )
    stacked = jnp.concatenate([hop0, hop1, hop2], 0)[:, order]
    arrived = lax.all_to_all(stacked, "dom", split_axis=1, concat_axis=1, tiled=True)
    placed = jnp.zeros_like(arrived).at[:, place].set(arrived)
    return placed.reshape(3, channels, node_count)


def solution(mesh):
    in_specs = (
        P(("dom", "rep"), None),
        P(),
        P("dom", None, None, None),
        P("dom", None),
        P("dom", None),
        P("dom", None),
        P("dom", None),
        P("dom", None),
    )
    out_specs = P(None, "rep", "dom")
    return jax.shard_map(
        on_device, mesh=mesh, in_specs=in_specs, out_specs=out_specs, check_vma=False
    )
```

profile of v0, /device:TPU:1, one launch (start us, length us, event | category | flops | bytes accessed | tf_op | source)
XLA Modules:
  0.0 156.7 jit_solution(11827091945666850877)
XLA Ops:
  1.1 2.1 %convolution_convert_fusion = bf16[256,512]{1,0:T(8,128)(2,1)} fusion(bf16[768,256]{1,0:T(8,128)(2,1)} %param.9, bf16[512,768]{1,0:T(8,128)(2,1)S(1)} %copy-done), kind=kOutput, calls=%fused_computation.17 | convolution fusion | flops 201457664 | bytes 1441792 | tf_op jit(solution)/shard_map/dot_general | solution.py:10
  3.3 5.0 %all-to-all-start = ((bf16[4,64,512]{2,1,0:T(8,128)(2,1)}), bf16[4,64,512]{2,1,0:T(8,128)(2,1)S(1)}, u32[]{:S(2)}, u32[]{:S(2)}) async-start(bf16[4,64,512]{2,1,0:T(8,128)(2,1)} %bitcast.2), calls=%async_computation | async-start | bytes 524288 | tf_op jit(solution)/shard_map/all_to_all | solution.py:13
  8.2 2.5 %convert_reduce_fusion = f32[20,256]{1,0:T(8,128)S(1)} fusion(bf16[1,20,256,256]{3,2,1,0:T(8,128)(2,1)} %param.10), kind=kLoop, calls=%fused_computation.6 | loop fusion | flops 2616320 | bytes 2641920 | tf_op jit(solution)/shard_map/reduce_sum | solution.py:26
  10.9 2.9 %all-to-all-done = bf16[4,64,512]{2,1,0:T(8,128)(2,1)S(1)} async-done(((bf16[4,64,512]{2,1,0:T(8,128)(2,1)}), bf16[4,64,512]{2,1,0:T(8,128)(2,1)S(1)}, u32[]{:S(2)}, u32[]{:S(2)}) %all-to-all-start) | async-done | bytes 262176 | tf_op jit(solution)/shard_map/all_to_all | solution.py:13
  14.1 3.2 %gather_fusion = bf16[1024,64]{1,0:T(8,128)(2,1)S(1)} fusion(bf16[64,2048]{0,1:T(8,128)(2,1)S(1)} %copy.38, s32[1024]{0:T(1024)S(1)} %broadcast_clamp_fusion.1), kind=kCustom, calls=%fused_computation | custom fusion | bytes 266240 | tf_op jit(solution)/shard_map/gather | solution.py:40
  18.2 19.0 %all-to-all-start.1 = ((bf16[128,2,256]{2,1,0:T(2,128)(2,1)}), bf16[128,2,256]{2,1,0:T(2,128)(2,1)S(1)}, u32[]{:S(2)}, u32[]{:S(2)}) async-start(bf16[128,2,256]{2,1,0:T(2,128)(2,1)} %reshape.194), calls=%async_computation.1 | async-start | bytes 262144 | tf_op jit(solution)/shard_map/all_to_all | solution.py:40
  37.3 12.7 %all-to-all-done.1 = bf16[128,2,256]{2,1,0:T(2,128)(2,1)S(1)} async-done(((bf16[128,2,256]{2,1,0:T(2,128)(2,1)}), bf16[128,2,256]{2,1,0:T(2,128)(2,1)S(1)}, u32[]{:S(2)}, u32[]{:S(2)}) %all-to-all-start.1) | async-done | bytes 131104 | tf_op jit(solution)/shard_map/all_to_all | solution.py:40
  52.3 2.5 %gather_fusion.1 = bf16[20,64,256]{2,1,0:T(8,128)(2,1)} fusion(bf16[64,12,256]{2,0,1:T(8,128)(2,1)} %bitcast.93, s32[1024]{0:T(1024)S(1)} %pad_clamp_fusion), kind=kCustom, calls=%fused_computation.1 | custom fusion | bytes 1310800 | tf_op jit(solution)/shard_map/gather | solution.py:33
  54.7 2.0 %fusion.8 = f32[64,20,256]{2,0,1:T(8,128)S(1)} fusion(bf16[1,20,256,256]{3,2,1,0:T(8,128)(2,1)S(1)} %copy-done.1, bf16[20,64,256]{2,1,0:T(8,128)(2,1)} %gather_fusion.1), kind=kOutput, calls=%fused_computation.15 | convolution fusion | flops 167772160 | bytes 4587520 | tf_op jit(solution)/shard_map/ctj,tij->cti/dot_general | solution.py:34
  56.7 1.3 fusion.6
  59.0 2.0 %copy.42 = bf16[64,2048]{0,1:T(8,128)(2,1)} copy(bf16[64,2048]{1,0:T(8,128)(2,1)} %divide_convert_fusion.1) | data formatting | bytes 524288 | tf_op jit(solution)/shard_map/convert_element_type | solution.py:37
  60.9 5.1 %gather_fusion.2 = bf16[1024,64]{1,0:T(8,128)(2,1)} fusion(bf16[64,2048]{0,1:T(8,128)(2,1)} %copy.42, s32[1024]{0:T(1024)S(1)} %broadcast_clamp_fusion.1), kind=kCustom, calls=%fused_computation.2 | custom fusion | bytes 266240 | tf_op jit(solution)/shard_map/gather | solution.py:43
  66.1 1.7 %bitcast_bitcast_fusion.2 = bf16[128,8,64]{2,1,0:T(8,128)(2,1)} fusion(bf16[1024,64]{1,0:T(8,128)(2,1)} %gather_fusion.2), kind=kLoop, calls=%fused_computation.45 | loop fusion | bytes 262144
  67.7 1.8 %reshape.196 = bf16[128,2,256]{2,1,0:T(2,128)(2,1)} reshape(bf16[128,8,64]{2,1,0:T(8,128)(2,1)} %bitcast_bitcast_fusion.2) | data formatting | bytes 262144
  69.6 5.5 %all-to-all-start.2 = ((bf16[128,2,256]{2,1,0:T(2,128)(2,1)}), bf16[128,2,256]{2,1,0:T(2,128)(2,1)S(1)}, u32[]{:S(2)}, u32[]{:S(2)}) async-start(bf16[128,2,256]{2,1,0:T(2,128)(2,1)} %reshape.196), calls=%async_computation.2 | async-start | bytes 262144 | tf_op jit(solution)/shard_map/all_to_all | solution.py:43
  75.9 12.1 %all-to-all-done.2 = bf16[128,2,256]{2,1,0:T(2,128)(2,1)S(1)} async-done(((bf16[128,2,256]{2,1,0:T(2,128)(2,1)}), bf16[128,2,256]{2,1,0:T(2,128)(2,1)S(1)}, u32[]{:S(2)}, u32[]{:S(2)}) %all-to-all-start.2) | async-done | bytes 131104 | tf_op jit(solution)/shard_map/all_to_all | solution.py:43
  88.9 1.7 %bitcast_bitcast_fusion = bf16[64,1024]{0,1:T(8,128)(2,1)} fusion(bf16[128,8,64]{2,1,0:T(8,128)(2,1)} %reshape.197), kind=kLoop, calls=%fused_computation.43 | loop fusion | bytes 262144 | tf_op jit(solution)/shard_map/all_to_all | solution.py:43
  93.4 2.6 %gather_fusion.3 = bf16[20,64,256]{2,1,0:T(8,128)(2,1)} fusion(bf16[64,12,256]{2,0,1:T(8,128)(2,1)} %bitcast.92, s32[1024]{0:T(1024)} %copy-done.6), kind=kCustom, calls=%fused_computation.3 | custom fusion | bytes 1310800 | tf_op jit(solution)/shard_map/gather | solution.py:33
  96.0 2.0 %fusion.11 = f32[64,20,256]{2,0,1:T(8,128)S(1)} fusion(bf16[1,20,256,256]{3,2,1,0:T(8,128)(2,1)S(1)} %copy-done.1, bf16[20,64,256]{2,1,0:T(8,128)(2,1)} %gather_fusion.3), kind=kOutput, calls=%fused_computation.16 | convolution fusion | flops 167772160 | bytes 4587520 | tf_op jit(solution)/shard_map/ctj,tij->cti/dot_general | solution.py:34
  98.0 1.3 fusion.4
  100.2 9.0 %gather_fusion.4 = bf16[2048,192]{1,0:T(8,128)(2,1)} fusion(bf16[192,2048]{0,1:T(8,128)(2,1)S(1)} %copy.46, s32[2048]{0:T(1024)S(1)} %broadcast_clamp_fusion), kind=kCustom, calls=%fused_computation.4 | custom fusion | bytes 1581056 | tf_op jit(solution)/shard_map/gather | solution.py:45
  109.2 5.7 %all-to-all-start.3 = ((bf16[192,128,16]{0,2,1:T(8,128)(2,1)}), bf16[192,128,16]{0,2,1:T(8,128)(2,1)S(1)}, u32[]{:S(2)}, u32[]{:S(2)}) async-start(bf16[192,128,16]{0,2,1:T(8,128)(2,1)} %bitcast.26), calls=%async_computation.3 | async-start | bytes 2097152 | tf_op jit(solution)/shard_map/all_to_all | solution.py:46
  114.9 31.0 %all-to-all-done.3 = bf16[192,128,16]{0,2,1:T(8,128)(2,1)S(1)} async-done(((bf16[192,128,16]{0,2,1:T(8,128)(2,1)}), bf16[192,128,16]{0,2,1:T(8,128)(2,1)S(1)}, u32[]{:S(2)}, u32[]{:S(2)}) %all-to-all-start.3) | async-done | bytes 786464 | tf_op jit(solution)/shard_map/all_to_all | solution.py:46
  145.9 9.6 %scatter_custom_fusion = bf16[192,2048]{0,1:T(8,128)(2,1)S(1)} fusion(s32[2048]{0:T(1024)S(1)} %bitcast.106, bf16[2048,192]{1,0:T(8,128)(2,1)S(1)} %bitcast.100, bf16[]{:T(256)} %constant.5.clone.1), kind=kCustom, calls=%fused_computation.24 | custom fusion | bytes 786434 | tf_op jit(solution)/shard_map/scatter | solution.py:47
  (53 shorter events, 12.2 us)
Async XLA Ops:
  0.0 1.1 copy-start
  0.0 8.2 %copy-start.10 = (s32[1,1024]{1,0:T(1,128)S(1)}, s32[1,1024]{1,0:T(1,128)}, u32[]{:S(2)}) copy-start(s32[1,1024]{1,0:T(1,128)} %param.13) | copy-start | bytes 12292
  3.3 7.5 %copy-start.7 = (s32[1,20]{1,0:T(1,128)S(1)}, s32[1,20]{1,0:T(1,128)}, u32[]{:S(2)}) copy-start(s32[1,20]{1,0:T(1,128)} %param.11) | copy-start | bytes 244
  3.3 10.5 %all-to-all-start = ((bf16[4,64,512]{2,1,0:T(8,128)(2,1)}), bf16[4,64,512]{2,1,0:T(8,128)(2,1)S(1)}, u32[]{:S(2)}, u32[]{:S(2)}) async-start(bf16[4,64,512]{2,1,0:T(8,128)(2,1)} %bitcast.2), calls=%async_computation | async-start | bytes 524288 | tf_op jit(solution)/shard_map/all_to_all | solution.py:13
  13.8 4.4 %copy-start.3 = (bf16[4,8,8,512]{3,2,0,1:T(8,128)(2,1)}, bf16[4,8,8,512]{3,2,0,1:T(8,128)(2,1)S(1)}, u32[]{:S(2)}) copy-start(bf16[4,8,8,512]{3,2,0,1:T(8,128)(2,1)S(1)} %copy.50) | copy-start | bytes 786436
  13.8 23.4 %copy-start.11 = (s32[1,20]{1,0:T(1,128)S(1)}, s32[1,20]{1,0:T(1,128)}, u32[]{:S(2)}) copy-start(s32[1,20]{1,0:T(1,128)} %param.12) | copy-start | bytes 244
  18.2 31.8 %all-to-all-start.1 = ((bf16[128,2,256]{2,1,0:T(2,128)(2,1)}), bf16[128,2,256]{2,1,0:T(2,128)(2,1)S(1)}, u32[]{:S(2)}, u32[]{:S(2)}) async-start(bf16[128,2,256]{2,1,0:T(2,128)(2,1)} %reshape.194), calls=%async_computation.1 | async-start | bytes 262144 | tf_op jit(solution)/shard_map/all_to_all | solution.py:40
  37.3 17.5 %copy-start.6 = (s32[1024]{0:T(1024)}, s32[1024]{0:T(1024)S(1)}, u32[]{:S(2)}) copy-start(s32[1024]{0:T(1024)S(1)} %pad_clamp_fusion) | copy-start | bytes 12292
  50.3 4.4 %copy-start.1 = (bf16[1,20,256,256]{3,2,1,0:T(8,128)(2,1)S(1)}, bf16[1,20,256,256]{3,2,1,0:T(8,128)(2,1)}, u32[]{:S(2)}) copy-start(bf16[1,20,256,256]{3,2,1,0:T(8,128)(2,1)} %param.10) | copy-start | bytes 7864324
  54.7 2.0 %copy-start.8 = (s32[1,20]{1,0:T(1,128)S(1)}, s32[1,20]{1,0:T(1,128)}, u32[]{:S(2)}) copy-start(s32[1,20]{1,0:T(1,128)} %param.11) | copy-start | bytes 244
  69.6 18.4 %all-to-all-start.2 = ((bf16[128,2,256]{2,1,0:T(2,128)(2,1)}), bf16[128,2,256]{2,1,0:T(2,128)(2,1)S(1)}, u32[]{:S(2)}, u32[]{:S(2)}) async-start(bf16[128,2,256]{2,1,0:T(2,128)(2,1)} %reshape.196), calls=%async_computation.2 | async-start | bytes 262144 | tf_op jit(solution)/shard_map/all_to_all | solution.py:43
  96.0 2.0 %copy-start.9 = (s32[1,20]{1,0:T(1,128)S(1)}, s32[1,20]{1,0:T(1,128)}, u32[]{:S(2)}) copy-start(s32[1,20]{1,0:T(1,128)} %param.11) | copy-start | bytes 244
  98.0 1.6 %copy-start.2 = (bf16[64,2048]{1,0:T(8,128)(2,1)S(1)}, bf16[64,2048]{1,0:T(8,128)(2,1)}, u32[]{:S(2)}) copy-start(bf16[64,2048]{1,0:T(8,128)(2,1)} %divide_convert_fusion.1) | copy-start | bytes 786436
  98.0 1.6 %copy-start.4 = (bf16[4,8,8,512]{3,2,0,1:T(8,128)(2,1)S(1)}, bf16[4,8,8,512]{3,2,0,1:T(8,128)(2,1)}, u32[]{:S(2)}) copy-start(bf16[4,8,8,512]{3,2,0,1:T(8,128)(2,1)} %copy-done.3) | copy-start | bytes 786436
  109.2 5.7 %copy-start.5 = (s32[1,2048]{1,0:T(1,128)S(1)}, s32[1,2048]{1,0:T(1,128)}, u32[]{:S(2)}) copy-start(s32[1,2048]{1,0:T(1,128)} %param.15) | copy-start | bytes 24580
  109.2 36.7 %all-to-all-start.3 = ((bf16[192,128,16]{0,2,1:T(8,128)(2,1)}), bf16[192,128,16]{0,2,1:T(8,128)(2,1)S(1)}, u32[]{:S(2)}, u32[]{:S(2)}) async-start(bf16[192,128,16]{0,2,1:T(8,128)(2,1)} %bitcast.26), calls=%async_computation.3 | async-start | bytes 2097152 | tf_op jit(solution)/shard_map/all_to_all | solution.py:46
where the time goes:
time: 158 us; the launch traced here: 157 us
  waiting for transfers between devices  58.6 us (37%)
  local copies, waits for them, and re-layouts  47.4 us (30%)
  starting transfers between devices  35.3 us (22%)
  matrix products  8.87 us (6%)
  other arithmetic  6.19 us (4%)
    all_to_all x1, waiting for transfers between devices, on_device(): lax.all_to_all(stacked, 'dom', split_axis=1, concat_axis=1, tiled=True)  31 us
    all_to_all x1, starting transfers between devices, on_device(): lax.all_to_all(hop0[:, halo_rows], 'dom', split_axis=1, concat_axis=1, ti...  19 us
    all_to_all x1, waiting for transfers between devices, on_device(): lax.all_to_all(hop0[:, halo_rows], 'dom', split_axis=1, concat_axis=1, ti...  12.7 us
    all_to_all x1, waiting for transfers between devices, on_device(): lax.all_to_all(hop1[:, halo_rows], 'dom', split_axis=1, concat_axis=1, ti...  12.1 us
    scatter x2, local copies, waits for them, and re-layouts, on_device(): placed = jnp.zeros_like(arrived).at[:, place].set(arrived)  10.8 us
    gather x1, local copies, waits for them, and re-layouts, on_device(): stacked = jnp.concatenate([hop0, hop1, hop2], 0)[:, order]  8.98 us
    unnamed x33, local copies, waits for them, and re-layouts  7.05 us
    all_to_all x1, starting transfers between devices, on_device(): lax.all_to_all(stacked, 'dom', split_axis=1, concat_axis=1, tiled=True)  5.71 us
  transfers between devices with their start and end apart: 4, of which 4 were waited for; matrix products, arithmetic and copies ran while one was open for 2% of the time, Pallas kernels for 0%

commit v1 on v0

v1 whole, which is shorter than its diff:
```python
import jax
import jax.numpy as jnp
from jax import lax
from jax.experimental import pallas as pl
from jax.experimental.pallas import tpu as pltpu
from jax.sharding import PartitionSpec as P

MESH = pl.DeviceIdType.MESH
BF16, F32, I32 = jnp.bfloat16, jnp.float32, jnp.int32
NZ = 8
NA = 16
NREP = 4
CH = 64
NT = 20
HALF = 128

REP, HALO1, HALO2, LAY1, LAY2 = 0, 1, 3, 5, 8


def dot_nt(a, b):
    return lax.dot_general(a, b, (((1,), (1,)), ((), ())), preferred_element_type=F32)


def dot_nn(a, b):
    return lax.dot_general(a, b, (((1,), (0,)), ((), ())), preferred_element_type=F32)


def build(ref, chunk, idx, rows):
    step = 64
    width = idx.shape[1]

    def body(r, _):
        base = pl.multiple_of(r * step, step)
        row = lax.broadcasted_iota(I32, (step, width), 0)
        hot = jnp.where(row == idx - base, 1.0, 0.0).astype(BF16)
        ref[chunk, pl.ds(base, step), :] = hot
        return 0

    lax.fori_loop(0, rows // step, body, 0)


def kernel(
    feat, sketch, tiles, tdst, tsrc, hidx, oidx, pidx, out,
    fbuf, sbuf, tbuf, c0, c1, c2, rs, hs, hr, ub, ts, ls, lr, ls2, arr,
    ohh, ohl, ohp, permh, perml, prods, invd, lsem, ssem, rsem,
):
    dom = lax.axis_index("dom")
    rep = lax.axis_index("rep")
    z = dom // NA
    a = dom % NA
    layers = (c0, c1, c2)

    load_f = pltpu.make_async_copy(feat, fbuf, lsem.at[0])
    load_s = pltpu.make_async_copy(sketch, sbuf, lsem.at[1])
    load_t = pltpu.make_async_copy(tiles, tbuf, lsem.at[2])
    load_s.start()
    load_f.start()
    load_t.start()

    barrier = pltpu.get_barrier_semaphore()

    def greet(o, _):
        pl.semaphore_signal(
            barrier, inc=1, device_id=(z * NA + (a + o) % NA, rep), device_id_type=MESH
        )
        return 0

    def greet_z(o, _):
        pl.semaphore_signal(
            barrier, inc=1, device_id=((z + o) % NZ * NA + a, rep), device_id_type=MESH
        )
        return 0

    def greet_rep(o, _):
        pl.semaphore_signal(
            barrier, inc=1, device_id=(dom, (rep + o) % NREP), device_id_type=MESH
        )
        return 0

    lax.fori_loop(1, NREP, greet_rep, 0)
    lax.fori_loop(1, NA, greet, 0)
    lax.fori_loop(1, NZ, greet_z, 0)

    load_s.wait()
    st = sbuf[...].T
    load_f.wait()
    for h in range(2):
        y = dot_nt(st, fbuf[h * 256 : (h + 1) * 256, :]).astype(BF16)
        for r in range(NREP):
            for k in range(2):
                rs[r, 2 * h + k] = y[r * CH : (r + 1) * CH, k * HALF : (k + 1) * HALF]

    pl.semaphore_wait(barrier, NREP - 1 + NA - 1 + NZ - 1)

    mine = c0.at[pl.ds(rep * 4, 4)]

    def send_rep(o, _):
        to = (rep + o) % NREP
        pltpu.make_async_remote_copy(
            src_ref=rs.at[to], dst_ref=mine, send_sem=ssem.at[REP], recv_sem=rsem.at[REP],
            device_id=(dom, to), device_id_type=MESH,
        ).start()
        return 0

    lax.fori_loop(1, NREP, send_rep, 0)
    pltpu.make_async_copy(rs.at[rep], mine, rsem.at[REP]).start()

    def wait_on(ref, sem):
        pltpu.make_async_copy(ref, ref, sem).wait()

    def send_a(src, dst, row, to):
        @pl.when(to != a)
        def _():
            pltpu.make_async_remote_copy(
                src_ref=src.at[to], dst_ref=dst.at[a], send_sem=ssem.at[row],
                recv_sem=rsem.at[row], device_id=(z * NA + to, rep), device_id_type=MESH,
            ).start()

        @pl.when(to == a)
        def _():
            pltpu.make_async_copy(src.at[to], dst.at[a], rsem.at[row]).start()

    def send_z(src, dst, row, to):
        @pl.when(to != z)
        def _():
            pltpu.make_async_remote_copy(
                src_ref=src.at[to], dst_ref=dst.at[z], send_sem=ssem.at[row],
                recv_sem=rsem.at[row], device_id=(to * NA + a, rep), device_id_type=MESH,
            ).start()

        @pl.when(to == z)
        def _():
            pltpu.make_async_copy(src.at[to], dst.at[z], rsem.at[row]).start()

    def local_cols(c):
        return jnp.concatenate([c[i] for i in range(16)], axis=1)

    low = lax.broadcasted_iota(I32, (32, HALF), 1) < CH

    def halo_start(k):
        c = layers[k]

        def body(i, _):
            chunk = (a // 4 + 2 + i) % 4
            g = dot_nn(local_cols(c), ohh[chunk])
            for p in range(2):
                top = g[0:32, p * HALF : (p + 1) * HALF]
                bot = g[32:64, p * HALF : (p + 1) * HALF]
                hs[k, chunk * 4 + 2 * p] = jnp.where(low, top, pltpu.roll(bot, CH, 1)).astype(BF16)
                hs[k, chunk * 4 + 2 * p + 1] = jnp.where(low, pltpu.roll(top, CH, 1), bot).astype(BF16)
            for j in range(4):
                send_a(hs.at[k], hr.at[k], HALO1 + k, chunk * 4 + j)
            return 0

        lax.fori_loop(0, 4, body, 0)

    def halo_turn(k):
        wait_on(hr.at[k], rsem.at[HALO1 + k])
        for q in range(8):
            r0 = hr[k, 2 * q].astype(F32)
            r1 = hr[k, 2 * q + 1].astype(F32)
            ub[0:32, q * HALF : (q + 1) * HALF] = jnp.where(low, r0, pltpu.roll(r1, CH, 1)).astype(BF16)
            ub[32:64, q * HALF : (q + 1) * HALF] = jnp.where(low, pltpu.roll(r0, CH, 1), r1).astype(BF16)
        dst = layers[k].at[pl.ds(16, NZ)]

        def body(i, _):
            chunk = (z // 2 + 2 + i) % 4
            t = dot_nn(ub[...], permh[chunk]).astype(BF16)
            for p in range(2):
                ts[k, chunk * 2 + p] = t[:, p * HALF : (p + 1) * HALF]
            for p in range(2):
                send_z(ts.at[k], dst, HALO2 + k, chunk * 2 + p)
            return 0

        lax.fori_loop(0, 4, body, 0)

    def layout_start(k):
        c = layers[k]

        def body(i, _):
            chunk = (a // 2 + 4 + i) % 8
            g = dot_nn(local_cols(c), ohl[chunk]).astype(BF16)
            for p in range(2):
                ls[k, chunk * 2 + p] = g[:, p * HALF : (p + 1) * HALF]
            for p in range(2):
                send_a(ls.at[k], lr.at[k], LAY1 + k, chunk * 2 + p)
            return 0

        lax.fori_loop(0, 8, body, 0)

    def layout_turn(k):
        wait_on(lr.at[k], rsem.at[LAY1 + k])

        def body(i, _):
            chunk = (z // 2 + 2 + i) % 4
            x = jnp.concatenate(
                [jnp.concatenate([lr[k, g * 8 + j] for j in range(8)], axis=1) for g in range(2)],
                axis=0,
            )
            t = dot_nn(x, perml[chunk]).astype(BF16)
            for p in range(2):
                for g in range(2):
                    ls2[k, chunk * 2 + p, g] = t[g * CH : (g + 1) * CH, p * HALF : (p + 1) * HALF]
            for p in range(2):
                send_z(ls2.at[k], arr.at[k], LAY2 + k, chunk * 2 + p)
            return 0

        lax.fori_loop(0, 4, body, 0)

    def product(c, t, s):
        x = jnp.concatenate([c[2 * s], c[2 * s + 1]], axis=1)
        prods[t] = dot_nt(x, tbuf[t])

    def combine_local(k):
        def body(t, _):
            product(layers[k], t, t)
            return 0

        lax.fori_loop(0, 8, body, 0)

    def mask(t, b):
        return jnp.where(tdst[0, t] == b, 1.0, 0.0).astype(F32)

    def combine_rest(k):
        wait_on(layers[k].at[pl.ds(16, NZ)], rsem.at[HALO2 + k])

        def body(t, _):
            product(layers[k], t, tsrc[0, t])
            return 0

        lax.fori_loop(8, NT, body, 0)
        nxt = layers[k + 1]

        def total(b, _):
            acc = prods[b]
            for t in range(8, NT):
                acc += mask(t, b) * prods[t]
            hop = (acc * invd[b][0:1, :]).astype(BF16)
            nxt[2 * b] = hop[:, :HALF]
            nxt[2 * b + 1] = hop[:, HALF:]
            return 0

        lax.fori_loop(0, 8, total, 0)

    def build_h(i, _):
        build(ohh, i, hidx[pl.ds(i, 1), :], 2048)
        return 0

    lax.fori_loop(0, 4, build_h, 0)
    load_t.wait()

    def row_sums(t, _):
        prods[t, 0:16, :] = dot_nt(jnp.ones((16, 256), BF16), tbuf[t])
        return 0

    lax.fori_loop(0, NT, row_sums, 0)

    def degrees(b, _):
        acc = prods[b, 0:8, :]
        for t in range(8, NT):
            acc += mask(t, b) * prods[t, 0:8, :]
        invd[b] = 1.0 / acc
        return 0

    lax.fori_loop(0, 8, degrees, 0)

    def build_ph(i, _):
        m = lax.broadcasted_iota(I32, (1, 256), 1) + i * 256
        build(permh, i, ((m >> 3) & 15) * 64 + (m >> 7) * 8 + (m & 7), 1024)
        return 0

    lax.fori_loop(0, 4, build_ph, 0)

    wait_on(c0.at[pl.ds(0, 16)], rsem.at[REP])
    halo_start(0)

    def build_l(i, _):
        build(ohl, i, oidx[pl.ds(i, 1), :], 2048)
        return 0

    lax.fori_loop(0, 8, build_l, 0)
    halo_turn(0)
    layout_start(0)
    combine_local(0)

    def build_pl(i, _):
        m = lax.broadcasted_iota(I32, (1, 256), 1) + i * 256
        build(perml, i, ((m >> 4) & 7) * 128 + (m >> 7) * 16 + (m & 15), 1024)
        return 0

    lax.fori_loop(0, 4, build_pl, 0)
    combine_rest(0)
    halo_start(1)
    layout_turn(0)
    halo_turn(1)
    layout_start(1)
    combine_local(1)

    def build_p(i, _):
        build(ohp, i, pidx[...] - i * 256, 256)
        return 0

    lax.fori_loop(0, 8, build_p, 0)
    combine_rest(1)
    layout_start(2)
    layout_turn(1)
    layout_turn(2)

    for k in range(3):
        wait_on(arr.at[k], rsem.at[LAY2 + k])

    def place(j, _):
        acc = jnp.zeros((3 * CH, 256), F32)
        for zz in range(NZ):
            x = jnp.concatenate(
                [jnp.concatenate([arr[k, zz, 0], arr[k, zz, 1]], axis=1) for k in range(3)], axis=0
            )
            acc += dot_nt(x, ohp[j, :, zz * 256 : (zz + 1) * 256])
        res = acc.astype(BF16)
        for k in range(3):
            out[k, :, pl.ds(pl.multiple_of(j * 256, 256), 256)] = res[k * CH : (k + 1) * CH]
        return 0

    lax.fori_loop(0, 8, place, 0)

    wait_on(rs.at[pl.ds(0, NREP - 1)], ssem.at[REP])
    for k in range(2):
        wait_on(hs.at[k, pl.ds(0, NA - 1)], ssem.at[HALO1 + k])
        wait_on(ts.at[k, pl.ds(0, NZ - 1)], ssem.at[HALO2 + k])
    for k in range(3):
        wait_on(ls.at[k, pl.ds(0, NA - 1)], ssem.at[LAY1 + k])
        wait_on(ls2.at[k, pl.ds(0, NZ - 1)], ssem.at[LAY2 + k])


def on_device(features, sketch_matrix, tiles, tile_dst, tile_src, halo_index, send_order, arrival_place):
    hidx = halo_index.reshape(NZ, NA, 8).transpose(1, 0, 2).reshape(4, 256)
    oidx = send_order.reshape(NZ, NA, 16).transpose(1, 0, 2).reshape(8, 256)
    vm, sm, hbm = (pl.BlockSpec(memory_space=s) for s in (pltpu.VMEM, pltpu.SMEM, pl.ANY))
    return pl.pallas_call(
        kernel,
        out_shape=jax.ShapeDtypeStruct((3, CH, 2048), BF16),
        in_specs=[hbm, hbm, hbm, sm, sm, vm, vm, vm],
        out_specs=vm,
        scratch_shapes=[
            pltpu.VMEM((512, 768), BF16),
            pltpu.VMEM((768, 256), BF16),
            pltpu.VMEM((NT, 256, 256), BF16),
            pltpu.VMEM((24, CH, HALF), BF16),
            pltpu.VMEM((24, CH, HALF), BF16),
            pltpu.VMEM((16, CH, HALF), BF16),
            pltpu.VMEM((NREP, 4, CH, HALF), BF16),
            pltpu.VMEM((2, NA, 32, HALF), BF16),
            pltpu.VMEM((2, NA, 32, HALF), BF16),
            pltpu.VMEM((CH, 1024), BF16),
            pltpu.VMEM((2, NZ, CH, HALF), BF16),
            pltpu.VMEM((3, NA, CH, HALF), BF16),
            pltpu.VMEM((3, NA, CH, HALF), BF16),
            pltpu.VMEM((3, NZ, 2, CH, HALF), BF16),
            pltpu.VMEM((3, NZ, 2, CH, HALF), BF16),
            pltpu.VMEM((4, 2048, 256), BF16),
            pltpu.VMEM((8, 2048, 256), BF16),
            pltpu.VMEM((8, 256, 2048), BF16),
            pltpu.VMEM((4, 1024, 256), BF16),
            pltpu.VMEM((4, 1024, 256), BF16),
            pltpu.VMEM((NT, CH, 256), F32),
            pltpu.VMEM((8, 8, 256), F32),
            pltpu.SemaphoreType.DMA((3,)),
            pltpu.SemaphoreType.DMA((11,)),
            pltpu.SemaphoreType.DMA((11,)),
        ],
        compiler_params=pltpu.CompilerParams(
            collective_id=0, has_side_effects=True, vmem_limit_bytes=56 * 2**20
        ),
    )(features, sketch_matrix, tiles[0], tile_dst, tile_src, hidx, oidx, arrival_place)


def solution(mesh):
    in_specs = (
        P(("dom", "rep"), None),
        P(),
        P("dom", None, None, None),
        P("dom", None),
        P("dom", None),
        P("dom", None),
        P("dom", None),
        P("dom", None),
    )
    return jax.shard_map(
        on_device, mesh=mesh, in_specs=in_specs, out_specs=P(None, "rep", "dom"), check_vma=False
    )
```

time: 158 us -> 82.6 us (0.52)
  Pallas kernels: 0 us -> 75.4 us
  waiting for transfers between devices: 58.6 us -> 0 us
  local copies, waits for them, and re-layouts: 47.4 us -> 4.18 us
  starting transfers between devices: 35.3 us -> 0 us
  matrix products: 8.87 us -> 0 us
  other arithmetic: 6.19 us -> 2.71 us
    pallas_call x0 -> x1, Pallas kernels: none -> 75.4 us  [on_device(): pl.pallas_call(kernel, out_shape=jax.ShapeDtypeStruct((3, CH, 2048), BF16...]
    all_to_all x4 -> x0, waiting for transfers between devices: 58.6 us -> none  [the longest x1 31 us: on_device(): lax.all_to_all(stacked, 'dom', split_axis=1, concat_axis=1, tiled=True)]
    all_to_all x4 -> x0, starting transfers between devices: 35.3 us -> none  [the longest x1 19 us: on_device(): lax.all_to_all(hop0[:, halo_rows], 'dom', split_axis=1, concat_axis=1, ti...]
    gather x5 -> x0, local copies, waits for them, and re-layouts: 22.4 us -> none  [the longest x1 8.98 us: on_device(): stacked = jnp.concatenate([hop0, hop1, hop2], 0)[:, order]]
    scatter x2 -> x0, local copies, waits for them, and re-layouts: 10.8 us -> none  [on_device(): placed = jnp.zeros_like(arrived).at[:, place].set(arrived)]
    dot_general x6 -> x0, matrix products: 8.87 us -> none  [the longest x2 4 us: combine(): jnp.einsum('ctj,tij->cti', blocks, tile_set, preferred_element_type=jnp.f...]
    unnamed x33 -> x2, local copies, waits for them, and re-layouts: 7.05 us -> 2.6 us
    all_to_all x6 -> x0, local copies, waits for them, and re-layouts: 3.17 us -> none  [the longest x2 2.73 us: on_device(): lax.all_to_all(hop1[:, halo_rows], 'dom', split_axis=1, concat_axis=1, ti...]
  transfers between devices with their start and end apart: 4 -> 0, of which waited for: 4 -> 0; matrix products, arithmetic and copies ran while one was open for 2% -> 0% of each run, Pallas kernels for 0% -> 0%
where the time goes in v1:
time: 82.6 us; the launch traced here: 82.3 us
  Pallas kernels  75.4 us (91%)
  local copies, waits for them, and re-layouts  4.18 us (5%)
  other arithmetic  2.71 us (3%)
    pallas_call x1, Pallas kernels, on_device(): pl.pallas_call(kernel, out_shape=jax.ShapeDtypeStruct((3, CH, 2048), BF16...  75.4 us
    unnamed x2, other arithmetic  2.71 us
    unnamed x2, local copies, waits for them, and re-layouts  2.6 us

profile of v1, /device:TPU:1, one launch (start us, length us, event | category | flops | bytes accessed | tf_op | source)
XLA Modules:
  0.0 82.3 jit_solution(1628978013487637683)
XLA Ops:
  0.0 0.5 broadcast.6
  0.5 1.3 %reduce.6 = s32[1024]{0:T(1024)S(1)} reduce(s32[1,1024]{1,0:T(1,128)} %param.13, s32[]{:T(128)} %broadcast.6), dimensions={0}, to_apply=%param.13.reduce_sub_computation.3 | reduce | bytes 8196 | tf_op args[5]
  1.9 1.4 %reduce.7 = s32[2048]{0:T(1024)S(1)} reduce(s32[1,2048]{1,0:T(1,128)} %param.14, s32[]{:T(128)} %broadcast.6), dimensions={0}, to_apply=%param.14.reduce_sub_computation.3 | reduce | bytes 16388 | tf_op args[6]
  3.2 0.1 reshape.14
  3.3 0.7 reshape.15.oidx
  4.0 0.1 reshape.12
  4.2 0.7 reshape.13.hidx
  4.8 75.4 %shard_map.82 = bf16[3,64,2048]{2,1,0:T(8,128)(2,1)} custom-call(bf16[512,768]{1,0:T(8,128)(2,1)} %feat.1, bf16[768,256]{1,0:T(8,128)(2,1)} %sketch.1, bf16[20,256,256]{2,1,0:T(8,128)(2,1)} %bitcast.5, s32[1,20]{1,0:T(1,128)} %tdst.1, s32[1,20]{1,0:T(1,128)} %tsrc.1, s32[4,256]{1,0:T(4,128)} %reshape.13.hidx, s32[8,256]{1,0:T(8,128)} %reshape.15.oidx, ...), custom_call_target="tpu_custom_call" | custom-call | tf_op jit(solution)/shard_map/pallas_call | solution.py:339
  80.2 2.1 %copy.16 = bf16[3,64,2048]{2,1,0:T(8,128)(2,1)} copy(bf16[3,64,2048]{2,1,0:T(8,128)(2,1)} %shard_map.82) | data formatting | bytes 1572864
  (2 shorter events, 0.0 us)

commit v2 on v1

--- a/solution.py
+++ b/solution.py
@@ -14,7 +14,7 @@
 NT = 20
 HALF = 128
 
-REP, HALO1, HALO2, LAY1, LAY2 = 0, 1, 3, 5, 8
+REP, HALO1, HALO2, LAY1, LAY2, LAST = 0, 1, 3, 5, 8, 11
 
 
 def dot_nt(a, b):
@@ -39,15 +39,41 @@
     lax.fori_loop(0, rows // step, body, 0)
 
 
+def far_first(i):
+    return jnp.where(i == 0, 2, jnp.where(i == 1, 1, jnp.where(i == 2, 3, 0)))
+
+
+def regroup(row, picks, width):
+    lane = lax.broadcasted_iota(I32, (1, HALF), 1)
+    out = jnp.zeros((1, HALF), I32)
+    for j, start in enumerate(picks):
+        base = start // HALF * HALF
+        piece = pltpu.roll(row[:, base : base + HALF], (j * width - (start - base)) % HALF, 1)
+        out = jnp.where(lane // width == j, piece, out)
+    return out
+
+
+def permute(x, perm):
+    return sum(dot_nt(x[:, c * 256 : (c + 1) * 256], perm[c]) for c in range(4))
+
+
+def halves(idx, first, second, row):
+    hi, lo = (idx >> 3).astype(F32), (idx & 7).astype(F32)
+    return jnp.where(row == first, hi, jnp.where(row == second, lo, 0.0))
+
+
 def kernel(
     feat, sketch, tiles, tdst, tsrc, hidx, oidx, pidx, out,
     fbuf, sbuf, tbuf, c0, c1, c2, rs, hs, hr, ub, ts, ls, lr, ls2, arr,
-    ohh, ohl, ohp, permh, perml, prods, invd, lsem, ssem, rsem,
+    ohh, ohl, ohp, permh, perml, hix, oix, pix, prods, total2, invd, lsem, ssem, rsem,
 ):
     dom = lax.axis_index("dom")
     rep = lax.axis_index("rep")
     z = dom // NA
     a = dom % NA
+    y = a // 2
+    core = a % 2
+    w = jnp.where(core == 0, z, y)
     layers = (c0, c1, c2)
 
     load_f = pltpu.make_async_copy(feat, fbuf, lsem.at[0])
@@ -66,9 +92,10 @@
         return 0
 
     def greet_z(o, _):
-        pl.semaphore_signal(
-            barrier, inc=1, device_id=((z + o) % NZ * NA + a, rep), device_id_type=MESH
-        )
+        for i in range(2):
+            pl.semaphore_signal(
+                barrier, inc=1, device_id=((z + o) % NZ * NA + y * 2 + i, rep), device_id_type=MESH
+            )
         return 0
 
     def greet_rep(o, _):
@@ -81,21 +108,34 @@
     lax.fori_loop(1, NA, greet, 0)
     lax.fori_loop(1, NZ, greet_z, 0)
 
+    def build_ph(i, _):
+        m = lax.broadcasted_iota(I32, (1, 256), 1) + i * 256
+        build(permh, i, ((m >> 3) & 15) * 64 + (m >> 7) * 8 + (m & 7), 1024)
+        return 0
+
+    lax.fori_loop(0, 4, build_ph, 0)
+
+    row16 = lax.broadcasted_iota(I32, (16, 1024), 0)
+    h = permute(halves(hidx[...], 0, 1, row16).astype(BF16), permh)
+    hp = (h[0:1] * 8.0 + h[1:2]).astype(I32)
+    for i in range(4):
+        hix[i : i + 1, :] = hp[:, i * 256 : (i + 1) * 256]
+
     load_s.wait()
     st = sbuf[...].T
     load_f.wait()
     for h in range(2):
-        y = dot_nt(st, fbuf[h * 256 : (h + 1) * 256, :]).astype(BF16)
+        hop = dot_nt(st, fbuf[h * 256 : (h + 1) * 256, :]).astype(BF16)
         for r in range(NREP):
             for k in range(2):
-                rs[r, 2 * h + k] = y[r * CH : (r + 1) * CH, k * HALF : (k + 1) * HALF]
-
-    pl.semaphore_wait(barrier, NREP - 1 + NA - 1 + NZ - 1)
+                rs[r, 2 * h + k] = hop[r * CH : (r + 1) * CH, k * HALF : (k + 1) * HALF]
+
+    pl.semaphore_wait(barrier, NREP - 1 + NA - 1 + 2 * (NZ - 1))
 
     mine = c0.at[pl.ds(rep * 4, 4)]
 
     def send_rep(o, _):
-        to = (rep + o) % NREP
+        to = (rep + jnp.where(o == 1, 2, jnp.where(o == 2, 1, 3))) % NREP
         pltpu.make_async_remote_copy(
             src_ref=rs.at[to], dst_ref=mine, send_sem=ssem.at[REP], recv_sem=rsem.at[REP],
             device_id=(dom, to), device_id_type=MESH,
@@ -132,6 +172,37 @@
         def _():
             pltpu.make_async_copy(src.at[to], dst.at[z], rsem.at[row]).start()
 
+    def send_first(k, m):
+        to = jnp.where(m < 8, z * NA + m * 2, (m - 8) * NA + y * 2 + 1)
+        slot = jnp.where(m < 8, a, z * 2 + core)
+        row = LAY1 + k
+
+        @pl.when(to != dom)
+        def _():
+            pltpu.make_async_remote_copy(
+                src_ref=ls.at[k, m], dst_ref=lr.at[k, slot], send_sem=ssem.at[row],
+                recv_sem=rsem.at[row], device_id=(to, rep), device_id_type=MESH,
+            ).start()
+
+        @pl.when(to == dom)
+        def _():
+            pltpu.make_async_copy(ls.at[k, m], lr.at[k, slot], rsem.at[row]).start()
+
+    def send_second(k, m):
+        to = jnp.where(core == 0, m * NA + a, z * NA + m * 2 + 1)
+        got = rsem.at[LAST + w] if k == 2 else rsem.at[LAY2 + k]
+
+        @pl.when(m != w)
+        def _():
+            pltpu.make_async_remote_copy(
+                src_ref=ls2.at[k, m], dst_ref=arr.at[k, w], send_sem=ssem.at[LAY2 + k],
+                recv_sem=got, device_id=(to, rep), device_id_type=MESH,
+            ).start()
+
+        @pl.when(m == w)
+        def _():
+            pltpu.make_async_copy(ls2.at[k, m], arr.at[k, w], got).start()
+
     def local_cols(c):
         return jnp.concatenate([c[i] for i in range(16)], axis=1)
 
@@ -141,7 +212,7 @@
         c = layers[k]
 
         def body(i, _):
-            chunk = (a // 4 + 2 + i) % 4
+            chunk = (a // 4 + far_first(i)) % 4
             g = dot_nn(local_cols(c), ohh[chunk])
             for p in range(2):
                 top = g[0:32, p * HALF : (p + 1) * HALF]
@@ -164,7 +235,7 @@
         dst = layers[k].at[pl.ds(16, NZ)]
 
         def body(i, _):
-            chunk = (z // 2 + 2 + i) % 4
+            chunk = (z // 2 + far_first(i)) % 4
             t = dot_nn(ub[...], permh[chunk]).astype(BF16)
             for p in range(2):
                 ts[k, chunk * 2 + p] = t[:, p * HALF : (p + 1) * HALF]
@@ -178,12 +249,13 @@
         c = layers[k]
 
         def body(i, _):
-            chunk = (a // 2 + 4 + i) % 8
+            off = far_first(i // 2)
+            chunk = jnp.where(i % 2 == 0, (y // 2 + off) % 4, 4 + (z // 2 + off) % 4)
             g = dot_nn(local_cols(c), ohl[chunk]).astype(BF16)
             for p in range(2):
                 ls[k, chunk * 2 + p] = g[:, p * HALF : (p + 1) * HALF]
             for p in range(2):
-                send_a(ls.at[k], lr.at[k], LAY1 + k, chunk * 2 + p)
+                send_first(k, chunk * 2 + p)
             return 0
 
         lax.fori_loop(0, 8, body, 0)
@@ -192,7 +264,7 @@
         wait_on(lr.at[k], rsem.at[LAY1 + k])
 
         def body(i, _):
-            chunk = (z // 2 + 2 + i) % 4
+            chunk = (w // 2 + far_first(i)) % 4
             x = jnp.concatenate(
                 [jnp.concatenate([lr[k, g * 8 + j] for j in range(8)], axis=1) for g in range(2)],
                 axis=0,
@@ -202,7 +274,7 @@
                 for g in range(2):
                     ls2[k, chunk * 2 + p, g] = t[g * CH : (g + 1) * CH, p * HALF : (p + 1) * HALF]
             for p in range(2):
-                send_z(ls2.at[k], arr.at[k], LAY2 + k, chunk * 2 + p)
+                send_second(k, chunk * 2 + p)
             return 0
 
         lax.fori_loop(0, 4, body, 0)
@@ -212,11 +284,12 @@
         prods[t] = dot_nt(x, tbuf[t])
 
     def combine_local(k):
-        def body(t, _):
-            product(layers[k], t, t)
-            return 0
-
-        lax.fori_loop(0, 8, body, 0)
+        def body(i, _):
+            for j in range(4):
+                product(layers[k], i * 4 + j, i * 4 + j)
+            return 0
+
+        lax.fori_loop(0, 2, body, 0)
 
     def mask(t, b):
         return jnp.where(tdst[0, t] == b, 1.0, 0.0).astype(F32)
@@ -224,11 +297,12 @@
     def combine_rest(k):
         wait_on(layers[k].at[pl.ds(16, NZ)], rsem.at[HALO2 + k])
 
-        def body(t, _):
-            product(layers[k], t, tsrc[0, t])
-            return 0
-
-        lax.fori_loop(8, NT, body, 0)
+        def body(i, _):
+            for j in range(4):
+                product(layers[k], i * 4 + j, tsrc[0, i * 4 + j])
+            return 0
+
+        lax.fori_loop(2, 5, body, 0)
         nxt = layers[k + 1]
 
         def total(b, _):
@@ -243,17 +317,43 @@
         lax.fori_loop(0, 8, total, 0)
 
     def build_h(i, _):
-        build(ohh, i, hidx[pl.ds(i, 1), :], 2048)
+        build(ohh, i, hix[pl.ds(i, 1), :], 2048)
         return 0
 
     lax.fori_loop(0, 4, build_h, 0)
+
+    def build_pl(i, _):
+        m = lax.broadcasted_iota(I32, (1, 256), 1) + i * 256
+        build(perml, i, ((m >> 4) & 7) * 128 + (m >> 7) * 16 + (m & 15), 1024)
+        return 0
+
+    lax.fori_loop(0, 4, build_pl, 0)
+    order = oidx[...]
+    for m in range(16):
+        if m < 8:
+            picks = [j * 256 + m * 32 for j in range(8)]
+        else:
+            picks = [(m - 8) * 256 + j * 32 + 16 for j in range(8)]
+        oix[m // 2 : m // 2 + 1, m % 2 * HALF : (m % 2 + 1) * HALF] = regroup(order, picks, 16)
+
+    wait_on(c0.at[pl.ds(0, 16)], rsem.at[REP])
+    halo_start(0)
+
+    def build_l(i, _):
+        build(ohl, i, oix[pl.ds(i, 1), :], 2048)
+        return 0
+
+    lax.fori_loop(0, 8, build_l, 0)
+    layout_start(0)
+    halo_turn(0)
     load_t.wait()
 
-    def row_sums(t, _):
-        prods[t, 0:16, :] = dot_nt(jnp.ones((16, 256), BF16), tbuf[t])
-        return 0
-
-    lax.fori_loop(0, NT, row_sums, 0)
+    def row_sums(i, _):
+        for j in range(4):
+            prods[i * 4 + j, 0:16, :] = dot_nt(jnp.ones((16, 256), BF16), tbuf[i * 4 + j])
+        return 0
+
+    lax.fori_loop(0, 5, row_sums, 0)
 
     def degrees(b, _):
         acc = prods[b, 0:8, :]
@@ -263,65 +363,60 @@
         return 0
 
     lax.fori_loop(0, 8, degrees, 0)
-
-    def build_ph(i, _):
-        m = lax.broadcasted_iota(I32, (1, 256), 1) + i * 256
-        build(permh, i, ((m >> 3) & 15) * 64 + (m >> 7) * 8 + (m & 7), 1024)
-        return 0
-
-    lax.fori_loop(0, 4, build_ph, 0)
-
-    wait_on(c0.at[pl.ds(0, 16)], rsem.at[REP])
-    halo_start(0)
-
-    def build_l(i, _):
-        build(ohl, i, oidx[pl.ds(i, 1), :], 2048)
-        return 0
-
-    lax.fori_loop(0, 8, build_l, 0)
-    halo_turn(0)
-    layout_start(0)
     combine_local(0)
 
-    def build_pl(i, _):
-        m = lax.broadcasted_iota(I32, (1, 256), 1) + i * 256
-        build(perml, i, ((m >> 4) & 7) * 128 + (m >> 7) * 16 + (m & 15), 1024)
-        return 0
-
-    lax.fori_loop(0, 4, build_pl, 0)
+    nat = pidx[...]
+    for m in range(16):
+        own = nat[:, m * HALF : (m + 1) * HALF]
+        picks = [(m % 2 * 4 + j) * 256 + m // 2 * 32 for j in range(4)]
+        turned = regroup(nat, picks, 32)
+        pix[m // 2 : m // 2 + 1, m % 2 * HALF : (m % 2 + 1) * HALF] = jnp.where(core == 0, own, turned)
+
+    def build_p(i, _):
+        build(ohp, i, pix[pl.ds(i, 1), :], 2048)
+        return 0
+
+    lax.fori_loop(0, 8, build_p, 0)
     combine_rest(0)
     halo_start(1)
     layout_turn(0)
+    layout_start(1)
     halo_turn(1)
-    layout_start(1)
     combine_local(1)
-
-    def build_p(i, _):
-        build(ohp, i, pidx[...] - i * 256, 256)
-        return 0
-
-    lax.fori_loop(0, 8, build_p, 0)
+    layout_turn(1)
     combine_rest(1)
     layout_start(2)
-    layout_turn(1)
+
+    def arrived(k, m):
+        return jnp.concatenate([arr[k, m, 0], arr[k, m, 1]], axis=1)
+
+    for k in range(2):
+        wait_on(arr.at[k], rsem.at[LAY2 + k])
+
+    def place(j, _):
+        rows = pl.ds(pl.multiple_of(j * 256, 256), 256)
+        acc = jnp.zeros((2 * CH, 256), F32)
+        for m in range(NZ):
+            x = jnp.concatenate([arrived(0, m), arrived(1, m)], axis=0)
+            acc += dot_nt(x, ohp[m, rows, :])
+        res = acc.astype(BF16)
+        for k in range(2):
+            out[k, :, rows] = res[k * CH : (k + 1) * CH]
+        return 0
+
+    lax.fori_loop(0, 8, place, 0)
     layout_turn(2)
-
-    for k in range(3):
-        wait_on(arr.at[k], rsem.at[LAY2 + k])
-
-    def place(j, _):
-        acc = jnp.zeros((3 * CH, 256), F32)
-        for zz in range(NZ):
-            x = jnp.concatenate(
-                [jnp.concatenate([arr[k, zz, 0], arr[k, zz, 1]], axis=1) for k in range(3)], axis=0
-            )
-            acc += dot_nt(x, ohp[j, :, zz * 256 : (zz + 1) * 256])
-        res = acc.astype(BF16)
-        for k in range(3):
-            out[k, :, pl.ds(pl.multiple_of(j * 256, 256), 256)] = res[k * CH : (k + 1) * CH]
-        return 0
-
-    lax.fori_loop(0, 8, place, 0)
+    total2[...] = jnp.zeros((CH, 2048), F32)
+
+    def place_last(i, _):
+        step = (i + 1) // 2
+        m = (w + jnp.where(i % 2 == 0, step, NZ - step)) % NZ
+        wait_on(arr.at[2, m], rsem.at[LAST + m])
+        total2[...] += dot_nt(arrived(2, m), ohp[m])
+        return 0
+
+    lax.fori_loop(0, NZ, place_last, 0)
+    out[2] = total2[...].astype(BF16)
 
     wait_on(rs.at[pl.ds(0, NREP - 1)], ssem.at[REP])
     for k in range(2):
@@ -333,8 +428,6 @@
 
 
 def on_device(features, sketch_matrix, tiles, tile_dst, tile_src, halo_index, send_order, arrival_place):
-    hidx = halo_index.reshape(NZ, NA, 8).transpose(1, 0, 2).reshape(4, 256)
-    oidx = send_order.reshape(NZ, NA, 16).transpose(1, 0, 2).reshape(8, 256)
     vm, sm, hbm = (pl.BlockSpec(memory_space=s) for s in (pltpu.VMEM, pltpu.SMEM, pl.ANY))
     return pl.pallas_call(
         kernel,
@@ -359,19 +452,23 @@
             pltpu.VMEM((3, NZ, 2, CH, HALF), BF16),
             pltpu.VMEM((4, 2048, 256), BF16),
             pltpu.VMEM((8, 2048, 256), BF16),
-            pltpu.VMEM((8, 256, 2048), BF16),
+            pltpu.VMEM((8, 2048, 256), BF16),
             pltpu.VMEM((4, 1024, 256), BF16),
             pltpu.VMEM((4, 1024, 256), BF16),
+            pltpu.VMEM((4, 256), I32),
+            pltpu.VMEM((8, 256), I32),
+            pltpu.VMEM((8, 256), I32),
             pltpu.VMEM((NT, CH, 256), F32),
+            pltpu.VMEM((CH, 2048), F32),
             pltpu.VMEM((8, 8, 256), F32),
             pltpu.SemaphoreType.DMA((3,)),
             pltpu.SemaphoreType.DMA((11,)),
-            pltpu.SemaphoreType.DMA((11,)),
+            pltpu.SemaphoreType.DMA((19,)),
         ],
         compiler_params=pltpu.CompilerParams(
             collective_id=0, has_side_effects=True, vmem_limit_bytes=56 * 2**20
         ),
-    )(features, sketch_matrix, tiles[0], tile_dst, tile_src, hidx, oidx, arrival_place)
+    )(features, sketch_matrix, tiles[0], tile_dst, tile_src, halo_index, send_order, arrival_place)
 
 
 def solution(mesh):

time: 82.6 us -> 70 us (0.85)
  Pallas kernels: 75.4 us -> 67.7 us
  other arithmetic: 2.71 us -> 0 us
  local copies, waits for them, and re-layouts: 4.18 us -> 2.09 us
    pallas_call x1, Pallas kernels: 75.4 us -> 67.7 us  [on_device(): pl.pallas_call(kernel, out_shape=jax.ShapeDtypeStruct((3, CH, 2048), BF16...]
    unnamed x2 -> x0, other arithmetic: 2.71 us -> none
    reshape x5 -> x0, local copies, waits for them, and re-layouts: 1.55 us -> none  [the longest x3 0.79 us: on_device(): oidx = send_order.reshape(NZ, NA, 16).transpose(1, 0, 2).reshape(8, 256)]
    unnamed x2 -> x1, local copies, waits for them, and re-layouts: 2.6 us -> 2.09 us
where the time goes in v2:
time: 70 us; the launch traced here: 69.8 us
  Pallas kernels  67.7 us (97%)
  local copies, waits for them, and re-layouts  2.09 us (3%)
    pallas_call x1, Pallas kernels, on_device(): pl.pallas_call(kernel, out_shape=jax.ShapeDtypeStruct((3, CH, 2048), BF16...  67.7 us
    unnamed x1, local copies, waits for them, and re-layouts  2.09 us

profile of v2, /device:TPU:1, one launch (start us, length us, event | category | flops | bytes accessed | tf_op | source)
XLA Modules:
  0.0 69.8 jit_solution(4858650173881153279)
XLA Ops:
  0.0 67.7 %shard_map.82 = bf16[3,64,2048]{2,1,0:T(8,128)(2,1)} custom-call(bf16[512,768]{1,0:T(8,128)(2,1)} %feat.1, bf16[768,256]{1,0:T(8,128)(2,1)} %sketch.1, bf16[20,256,256]{2,1,0:T(8,128)(2,1)} %bitcast.1, s32[1,20]{1,0:T(1,128)} %tdst.1, s32[1,20]{1,0:T(1,128)} %tsrc.1, s32[1,1024]{1,0:T(1,128)} %hidx.1, s32[1,2048]{1,0:T(1,128)} %oidx.1, s32[1,2048]{1,0:T(1,128)} %pidx.1), custom_call_target="tpu_custom_call" | custom-call | tf_op jit(solution)/shard_map/pallas_call | solution.py:432
  67.7 2.1 %copy.10 = bf16[3,64,2048]{2,1,0:T(8,128)(2,1)} copy(bf16[3,64,2048]{2,1,0:T(8,128)(2,1)} %shard_map.82) | data formatting | bytes 1572864

commit v3 on v2

--- a/solution.py
+++ b/solution.py
@@ -108,19 +108,6 @@
     lax.fori_loop(1, NA, greet, 0)
     lax.fori_loop(1, NZ, greet_z, 0)
 
-    def build_ph(i, _):
-        m = lax.broadcasted_iota(I32, (1, 256), 1) + i * 256
-        build(permh, i, ((m >> 3) & 15) * 64 + (m >> 7) * 8 + (m & 7), 1024)
-        return 0
-
-    lax.fori_loop(0, 4, build_ph, 0)
-
-    row16 = lax.broadcasted_iota(I32, (16, 1024), 0)
-    h = permute(halves(hidx[...], 0, 1, row16).astype(BF16), permh)
-    hp = (h[0:1] * 8.0 + h[1:2]).astype(I32)
-    for i in range(4):
-        hix[i : i + 1, :] = hp[:, i * 256 : (i + 1) * 256]
-
     load_s.wait()
     st = sbuf[...].T
     load_f.wait()
@@ -245,12 +232,13 @@
 
         lax.fori_loop(0, 4, body, 0)
 
-    def layout_start(k):
+    def layout_start(k, only=None):
         c = layers[k]
 
         def body(i, _):
-            off = far_first(i // 2)
-            chunk = jnp.where(i % 2 == 0, (y // 2 + off) % 4, 4 + (z // 2 + off) % 4)
+            off = far_first(i // 2 if only is None else i)
+            over_y = i % 2 == 0 if only is None else only == "y"
+            chunk = jnp.where(over_y, (y // 2 + off) % 4, 4 + (z // 2 + off) % 4)
             g = dot_nn(local_cols(c), ohl[chunk]).astype(BF16)
             for p in range(2):
                 ls[k, chunk * 2 + p] = g[:, p * HALF : (p + 1) * HALF]
@@ -258,7 +246,7 @@
                 send_first(k, chunk * 2 + p)
             return 0
 
-        lax.fori_loop(0, 8, body, 0)
+        lax.fori_loop(0, 8 if only is None else 4, body, 0)
 
     def layout_turn(k):
         wait_on(lr.at[k], rsem.at[LAY1 + k])
@@ -315,6 +303,19 @@
             return 0
 
         lax.fori_loop(0, 8, total, 0)
+
+    def build_ph(i, _):
+        m = lax.broadcasted_iota(I32, (1, 256), 1) + i * 256
+        build(permh, i, ((m >> 3) & 15) * 64 + (m >> 7) * 8 + (m & 7), 1024)
+        return 0
+
+    lax.fori_loop(0, 4, build_ph, 0)
+
+    row16 = lax.broadcasted_iota(I32, (16, 1024), 0)
+    h = permute(halves(hidx[...], 0, 1, row16).astype(BF16), permh)
+    hp = (h[0:1] * 8.0 + h[1:2]).astype(I32)
+    for i in range(4):
+        hix[i : i + 1, :] = hp[:, i * 256 : (i + 1) * 256]
 
     def build_h(i, _):
         build(ohh, i, hix[pl.ds(i, 1), :], 2048)
@@ -344,8 +345,9 @@
         return 0
 
     lax.fori_loop(0, 8, build_l, 0)
-    layout_start(0)
+    layout_start(0, "z")
     halo_turn(0)
+    layout_start(0, "y")
     load_t.wait()
 
     def row_sums(i, _):
@@ -404,8 +406,9 @@
             out[k, :, rows] = res[k * CH : (k + 1) * CH]
         return 0
 
-    lax.fori_loop(0, 8, place, 0)
+    lax.fori_loop(0, 4, place, 0)
     layout_turn(2)
+    lax.fori_loop(4, 8, place, 0)
     total2[...] = jnp.zeros((CH, 2048), F32)
 
     def place_last(i, _):
@@ -431,7 +434,7 @@
     vm, sm, hbm = (pl.BlockSpec(memory_space=s) for s in (pltpu.VMEM, pltpu.SMEM, pl.ANY))
     return pl.pallas_call(
         kernel,
-        out_shape=jax.ShapeDtypeStruct((3, CH, 2048), BF16),
+        out_shape=pltpu.VMEM((3, CH, 2048), BF16),
         in_specs=[hbm, hbm, hbm, sm, sm, vm, vm, vm],
         out_specs=vm,
         scratch_shapes=[

time: 70 us -> 68 us (0.971)
  local copies, waits for them, and re-layouts: 2.09 us -> 0.88 us
  Pallas kernels: 67.7 us -> 66.9 us
    unnamed x1, local copies, waits for them, and re-layouts: 2.09 us -> 0.88 us
    pallas_call x1, Pallas kernels: 67.7 us -> 66.9 us  [on_device(): pl.pallas_call(kernel, out_shape=pltpu.VMEM((3, CH, 2048), BF16), in_spec...]
where the time goes in v3:
time: 68 us; the launch traced here: 67.8 us
  Pallas kernels  66.9 us (98%)
  local copies, waits for them, and re-layouts  0.88 us (1%)
    pallas_call x1, Pallas kernels, on_device(): pl.pallas_call(kernel, out_shape=pltpu.VMEM((3, CH, 2048), BF16), in_spec...  66.9 us

profile of v3, /device:TPU:1, one launch (start us, length us, event | category | flops | bytes accessed | tf_op | source)
XLA Modules:
  0.0 67.8 jit_solution(3132362490273045090)
XLA Ops:
  0.0 66.9 %shard_map.82 = bf16[3,64,2048]{2,1,0:T(8,128)(2,1)S(1)} custom-call(bf16[512,768]{1,0:T(8,128)(2,1)} %feat.1, bf16[768,256]{1,0:T(8,128)(2,1)} %sketch.1, bf16[20,256,256]{2,1,0:T(8,128)(2,1)} %bitcast.1, s32[1,20]{1,0:T(1,128)} %tdst.1, s32[1,20]{1,0:T(1,128)} %tsrc.1, s32[1,1024]{1,0:T(1,128)} %hidx.1, s32[1,2048]{1,0:T(1,128)} %oidx.1, s32[1,2048]{1,0:T(1,128)} %pidx.1), custom_call_target="tpu_custom_call" | custom-call | tf_op jit(solution)/shard_map/pallas_call | solution.py:435
  67.0 0.9 %copy.10 = bf16[3,64,2048]{2,1,0:T(8,128)(2,1)} copy(bf16[3,64,2048]{2,1,0:T(8,128)(2,1)S(1)} %shard_map.82) | data formatting | bytes 1572864

commit v4 on v3

--- a/solution.py
+++ b/solution.py
@@ -76,12 +76,15 @@
     w = jnp.where(core == 0, z, y)
     layers = (c0, c1, c2)
 
-    load_f = pltpu.make_async_copy(feat, fbuf, lsem.at[0])
+    load_f = [
+        pltpu.make_async_copy(feat.at[rows], fbuf.at[rows], lsem.at[sem])
+        for rows, sem in ((pl.ds(0, 256), 0), (pl.ds(256, 256), 3))
+    ]
     load_s = pltpu.make_async_copy(sketch, sbuf, lsem.at[1])
     load_t = pltpu.make_async_copy(tiles, tbuf, lsem.at[2])
     load_s.start()
-    load_f.start()
-    load_t.start()
+    for half in load_f:
+        half.start()
 
     barrier = pltpu.get_barrier_semaphore()
 
@@ -110,13 +113,14 @@
 
     load_s.wait()
     st = sbuf[...].T
-    load_f.wait()
     for h in range(2):
+        load_f[h].wait()
         hop = dot_nt(st, fbuf[h * 256 : (h + 1) * 256, :]).astype(BF16)
         for r in range(NREP):
             for k in range(2):
                 rs[r, 2 * h + k] = hop[r * CH : (r + 1) * CH, k * HALF : (k + 1) * HALF]
 
+    load_t.start()
     pl.semaphore_wait(barrier, NREP - 1 + NA - 1 + 2 * (NZ - 1))
 
     mine = c0.at[pl.ds(rep * 4, 4)]
@@ -464,7 +468,7 @@
             pltpu.VMEM((NT, CH, 256), F32),
             pltpu.VMEM((CH, 2048), F32),
             pltpu.VMEM((8, 8, 256), F32),
-            pltpu.SemaphoreType.DMA((3,)),
+            pltpu.SemaphoreType.DMA((4,)),
             pltpu.SemaphoreType.DMA((11,)),
             pltpu.SemaphoreType.DMA((19,)),
         ],

time: 68 us -> 68 us (level)
  no operation moved by 1% of the time
where the time goes in v4:
time: 68 us; the launch traced here: 67.8 us
  Pallas kernels  66.9 us (98%)
  local copies, waits for them, and re-layouts  0.88 us (1%)
    pallas_call x1, Pallas kernels, on_device(): pl.pallas_call(kernel, out_shape=pltpu.VMEM((3, CH, 2048), BF16), in_spec...  66.9 us

profile of v4, /device:TPU:1, one launch (start us, length us, event | category | flops | bytes accessed | tf_op | source)
XLA Modules:
  0.0 67.8 jit_solution(10412386072512772439)
XLA Ops:
  0.0 66.9 %shard_map.82 = bf16[3,64,2048]{2,1,0:T(8,128)(2,1)S(1)} custom-call(bf16[512,768]{1,0:T(8,128)(2,1)} %feat.1, bf16[768,256]{1,0:T(8,128)(2,1)} %sketch.1, bf16[20,256,256]{2,1,0:T(8,128)(2,1)} %bitcast.1, s32[1,20]{1,0:T(1,128)} %tdst.1, s32[1,20]{1,0:T(1,128)} %tsrc.1, s32[1,1024]{1,0:T(1,128)} %hidx.1, s32[1,2048]{1,0:T(1,128)} %oidx.1, s32[1,2048]{1,0:T(1,128)} %pidx.1), custom_call_target="tpu_custom_call" | custom-call | tf_op jit(solution)/shard_map/pallas_call | solution.py:439
  66.9 0.9 %copy.10 = bf16[3,64,2048]{2,1,0:T(8,128)(2,1)} copy(bf16[3,64,2048]{2,1,0:T(8,128)(2,1)S(1)} %shard_map.82) | data formatting | bytes 1572864

commit v5 on v3

--- a/solution.py
+++ b/solution.py
@@ -381,10 +381,10 @@
     lax.fori_loop(0, 8, build_p, 0)
     combine_rest(0)
     halo_start(1)
-    layout_turn(0)
     layout_start(1)
     halo_turn(1)
     combine_local(1)
+    layout_turn(0)
     layout_turn(1)
     combine_rest(1)
     layout_start(2)

time: 68 us -> 66.9 us (0.984)
  Pallas kernels: 66.9 us -> 65.9 us
    pallas_call x1, Pallas kernels: 66.9 us -> 65.9 us  [on_device(): pl.pallas_call(kernel, out_shape=pltpu.VMEM((3, CH, 2048), BF16), in_spec...]
where the time goes in v5:
time: 66.9 us; the launch traced here: 66.8 us
  Pallas kernels  65.9 us (99%)
  local copies, waits for them, and re-layouts  0.88 us (1%)
    pallas_call x1, Pallas kernels, on_device(): pl.pallas_call(kernel, out_shape=pltpu.VMEM((3, CH, 2048), BF16), in_spec...  65.9 us

profile of v5, /device:TPU:1, one launch (start us, length us, event | category | flops | bytes accessed | tf_op | source)
XLA Modules:
  0.0 66.8 jit_solution(7995145809287906709)
XLA Ops:
  0.0 65.9 %shard_map.82 = bf16[3,64,2048]{2,1,0:T(8,128)(2,1)S(1)} custom-call(bf16[512,768]{1,0:T(8,128)(2,1)} %feat.1, bf16[768,256]{1,0:T(8,128)(2,1)} %sketch.1, bf16[20,256,256]{2,1,0:T(8,128)(2,1)} %bitcast.1, s32[1,20]{1,0:T(1,128)} %tdst.1, s32[1,20]{1,0:T(1,128)} %tsrc.1, s32[1,1024]{1,0:T(1,128)} %hidx.1, s32[1,2048]{1,0:T(1,128)} %oidx.1, s32[1,2048]{1,0:T(1,128)} %pidx.1), custom_call_target="tpu_custom_call" | custom-call | tf_op jit(solution)/shard_map/pallas_call | solution.py:435
  65.9 0.9 %copy.10 = bf16[3,64,2048]{2,1,0:T(8,128)(2,1)} copy(bf16[3,64,2048]{2,1,0:T(8,128)(2,1)S(1)} %shard_map.82) | data formatting | bytes 1572864
